TPU v7x, 32 devices: a whole 2x2x4 slice. The times are simulated.
32 devices in a mesh: dp: 4 (over z), expert: 8 (over y, x, core).
Axes of the slice: x: 2, y: 2, z: 4, core: 2. Of those that a mesh axis runs over, the one named last changes fastest.
Arguments:
- tokens: bfloat16 [4096, 1024], P(('dp', 'expert')), may hold values from -6 to 6
- expert_ids: int32 [4096, 8], P(('dp', 'expert')), may hold values from 0 to 15, all different within a row; in each aligned block of 128 rows (0 to 127, 128 to 255, ...) at most 68 rows name the same one
- gate_values: float32 [4096, 8], P(('dp', 'expert')), may hold values from 0.05 to 0.5
- w_gate: bfloat16 [16, 1024, 384], P('expert', 'dp'), may hold values from -0.1875 to 0.1875
- w_up: bfloat16 [16, 1024, 384], P('expert', 'dp'), may hold values from -0.1875 to 0.1875
- w_down: bfloat16 [16, 384, 1024], P('expert', 'dp'), may hold values from -0.3125 to 0.3125
- partner: int32 [32], replicated, may hold values from 0 to 31, as said below
Outputs:
- contrast_loss: float32 [], replicated
- token_grad: bfloat16 [4096, 1024], P(('dp', 'expert'))
- gate_grad: float32 [4096, 8], P(('dp', 'expert'))
Inputs may be any that keep to these rules, and one draw needn't show every extreme that they name: `expert_ids`: each row names 8 different experts. Among the 128 rows of one sequence no expert is named more than 68 times, and in every draw some sequence names some expert exactly 68 times. partner[i] differs from i.
All inputs are finite; a program needn't handle non-finite values.
Results may differ from a plain program's by a relative error of at most 0.014.
Values may be sent and summed in bfloat16 or wider, within the bound.
A program may use at most 64 MiB of HBM per device.

v0:
```python
import jax
import jax.numpy as jnp
from jax import lax
from jax.sharding import PartitionSpec as P

score_scale = 20.0
highest = lax.Precision.HIGHEST


def silu_parts(pre_act):
    sigmoid_val = jax.nn.sigmoid(pre_act)
    return (pre_act * sigmoid_val, sigmoid_val * (1.0 + pre_act * (1.0 - sigmoid_val)))


def expert_forward(slot_piece, gate_full, up_full, down_full):
    pre_gate = jnp.einsum(
        "encd,edf->encf", slot_piece, gate_full, preferred_element_type=jnp.float32
    )
    pre_up = jnp.einsum("encd,edf->encf", slot_piece, up_full, preferred_element_type=jnp.float32)
    activated, derivative = silu_parts(pre_gate)
    hidden = (activated * pre_up).astype(jnp.bfloat16)
    expert_out = jnp.einsum(
        "encf,efd->encd", hidden, down_full, preferred_element_type=jnp.float32
    ).astype(jnp.bfloat16)
    return (expert_out, pre_gate, pre_up)


def on_device(tokens, expert_ids, gate_values, w_gate, w_up, w_down, partner):
    tok_rows, model_width = tokens.shape
    route_count = expert_ids.shape[1]
    local_experts = w_gate.shape[0]
    experts = lax.axis_size("expert") * local_experts
    capacity = tok_rows * route_count // experts + max(1, tok_rows * route_count // (16 * experts))
    slot_total = experts * capacity
    gate_full, up_full, down_full = (
        lax.all_gather(w_gate, "dp", axis=1, tiled=True),
        lax.all_gather(w_up, "dp", axis=1, tiled=True),
        lax.all_gather(w_down, "dp", axis=1, tiled=True),
    )
    expert_iota = jnp.arange(experts, dtype=jnp.int32)
    matches = expert_ids[:, :, None] == expert_iota
    chosen = jnp.sum(matches.astype(jnp.int32), axis=1, dtype=jnp.int32)
    chosen_gate = jnp.sum(jnp.where(matches, gate_values[:, :, None], 0.0), axis=1)
    before = jnp.cumsum(chosen, axis=0, dtype=jnp.int32) - chosen
    slot_rank = jnp.take_along_axis(before, expert_ids, axis=1)
    slot_row = (expert_ids * capacity + slot_rank).reshape(-1)
    slot_iota = jnp.arange(capacity, dtype=jnp.int32)
    onehot = (chosen.T[:, None, :] == 1) & (before.T[:, None, :] == slot_iota[None, :, None])
    placer = onehot.astype(jnp.bfloat16)
    slot_gate = jnp.sum(jnp.where(onehot, chosen_gate.T[:, None, :], 0.0), axis=2)
    outgoing = jnp.einsum("ect,td->ecd", placer, tokens, preferred_element_type=jnp.float32).astype(
        jnp.bfloat16
    )
    outgoing = outgoing.reshape(experts, 1, capacity, model_width)
    placer_flat = placer.reshape(slot_total, tok_rows)
    out_here, pre_gate, pre_up = expert_forward(
        lax.all_to_all(outgoing, "expert", split_axis=0, concat_axis=1, tiled=True),
        gate_full,
        up_full,
        down_full,
    )
    returned_out = lax.all_to_all(
        out_here, "expert", split_axis=1, concat_axis=0, tiled=True
    ).reshape(slot_total, model_width)
    weighted_sum = jnp.dot(
        slot_gate.reshape(slot_total), returned_out.astype(jnp.float32), precision=highest
    )
    pooled = jnp.mean(tokens.astype(jnp.float32), axis=0) + weighted_sum / tok_rows
    inv_rms = lax.rsqrt(jnp.mean(pooled * pooled) + 1e-06)
    embedding = (pooled * inv_rms).astype(jnp.bfloat16)[None, :]
    gathered = lax.all_gather(embedding, ("dp", "expert"), axis=0, tiled=True)
    batch_size = gathered.shape[0]
    own_index = lax.axis_index(("dp", "expert"))
    batch_iota = jnp.arange(batch_size, dtype=jnp.int32)
    scores = (
        score_scale
        / model_width
        * jnp.dot(gathered, embedding[0], preferred_element_type=jnp.float32)
    )
    others = batch_iota != own_index
    log_total = jnp.log(jnp.sum(jnp.where(others, jnp.exp(scores), 0.0)))
    own_partner = lax.dynamic_index_in_dim(partner, own_index, keepdims=False)
    partner_hit = (batch_iota == own_partner).astype(jnp.float32)
    weight = jnp.where(others, jnp.exp(scores - log_total), 0.0) - partner_hit
    all_embed = gathered.astype(jnp.float32)
    row_term = jnp.dot(weight, all_embed, precision=highest)
    all_totals = lax.all_gather(log_total[None], ("dp", "expert"), axis=0, tiled=True)
    column_weight = jnp.where(others, jnp.exp(scores - all_totals), 0.0) - (
        partner == own_index
    ).astype(jnp.float32)
    embed_grad = (
        score_scale
        / model_width
        * (row_term + jnp.dot(column_weight, all_embed, precision=highest))
    )
    partner_rows = jnp.take(gathered, partner, axis=0)
    partner_score = (
        score_scale
        / model_width
        * jnp.einsum("bd,bd->b", gathered, partner_rows, preferred_element_type=jnp.float32)
    )
    contrast_loss = jnp.mean(all_totals - partner_score)
    seq_grad = (
        inv_rms * embed_grad - inv_rms**3 * jnp.sum(pooled * embed_grad) / model_width * pooled
    )
    slot_dots = jnp.dot(returned_out.astype(jnp.float32), seq_grad, precision=highest)
    gate_grad = jnp.take(slot_dots, slot_row, axis=0).reshape(tok_rows, route_count)
    out_grad = (
        (slot_gate[:, :, None] * seq_grad)
        .astype(jnp.bfloat16)
        .reshape(experts, 1, capacity, model_width)
    )
    arrived = lax.all_to_all(out_grad, "expert", split_axis=0, concat_axis=1, tiled=True)
    hidden_grad = jnp.einsum(
        "encd,efd->encf", arrived, down_full, preferred_element_type=jnp.float32
    )
    activated, derivative = silu_parts(pre_gate)
    gate_side = (hidden_grad * pre_up * derivative).astype(jnp.bfloat16)
    up_side = (hidden_grad * activated).astype(jnp.bfloat16)
    route_here = jnp.einsum(
        "encf,edf->encd", gate_side, gate_full, preferred_element_type=jnp.float32
    )
    route_here = (
        route_here
        + jnp.einsum("encf,edf->encd", up_side, up_full, preferred_element_type=jnp.float32)
    ).astype(jnp.bfloat16)
    returned = lax.all_to_all(
        route_here, "expert", split_axis=1, concat_axis=0, tiled=True
    ).reshape(slot_total, model_width)
    route_sum = jnp.einsum("st,sd->td", placer_flat, returned, preferred_element_type=jnp.float32)
    token_grad = (seq_grad + route_sum).astype(jnp.bfloat16)
    return (contrast_loss, token_grad, gate_grad)


def solution(mesh):
    placed = (
        P(("dp", "expert"), None),
        P(("dp", "expert"), None),
        P(("dp", "expert"), None),
        P("expert", "dp", None),
        P("expert", "dp", None),
        P("expert", "dp", None),
        P(),
    )
    return jax.shard_map(
        on_device,
        mesh=mesh,
        in_specs=placed,
        out_specs=(P(), P(("dp", "expert"), None), P(("dp", "expert"), None)),
        check_vma=False,
    )
```

profile of v0, /device:TPU:0, one launch (start us, length us, event | category | flops | bytes accessed | tf_op | source)
XLA Modules:
  0.0 342.9 jit_solution(955340672697484617)
XLA Ops:
  9.7 3.1 convert_bitcast_fusion
  12.8 5.2 %all-to-all-start = ((bf16[16,1,68,1024]{3,2,1,0:T(8,128)(2,1)}), bf16[16,1,68,1024]{3,2,1,0:T(8,128)(2,1)S(1)}, u32[]{:S(2)}, u32[]{:S(2)}) async-start(bf16[16,1,68,1024]{3,2,1,0:T(8,128)(2,1)} %convert_bitcast_fusion), calls=%async_computation | async-start | bytes 4718592 | tf_op jit(solution)/shard_map/all_to_all | solution.py:57
  18.7 28.7 %all-to-all-done = bf16[16,1,68,1024]{3,2,1,0:T(8,128)(2,1)S(1)} async-done(((bf16[16,1,68,1024]{3,2,1,0:T(8,128)(2,1)}), bf16[16,1,68,1024]{3,2,1,0:T(8,128)(2,1)S(1)}, u32[]{:S(2)}, u32[]{:S(2)}) %all-to-all-start) | async-done | bytes 2228256 | tf_op jit(solution)/shard_map/all_to_all | solution.py:57
  47.5 1.9 all-gather.5.cloned.1.call-done
  49.4 4.0 %fusion.4 = f32[2,8,68,384]{3,2,1,0:T(8,128)} fusion(bf16[8,2,1,68,1024]{4,3,1,0,2:T(8,128)(2,1)S(1)} %bitcast.89, bf16[2,1024,384]{2,1,0:T(8,128)(2,1)} %all-gather.5.cloned.1.call-done), kind=kOutput, calls=%fused_computation.9 | convolution fusion | flops 855638016 | bytes 5472256 | tf_op jit(solution)/shard_map/encd,edf->encf/dot_general | solution.py:16
  53.4 33.5 %all-gather.7.cloned.1.call-done = bf16[2,1024,384]{2,1,0:T(8,128)(2,1)} async-done(((bf16[2,256,384]{2,1,0:T(8,128)(2,1)}), bf16[2,1024,384]{2,1,0:T(8,128)(2,1)}) %all-gather.7.cloned.1.call-update) | async-done | bytes 1572880 | tf_op jit(solution)/shard_map/all_gather | solution.py:37
  86.9 4.0 %fusion.2 = f32[2,8,68,384]{3,2,1,0:T(8,128)} fusion(bf16[8,2,1,68,1024]{4,3,1,0,2:T(8,128)(2,1)S(1)} %bitcast.90, bf16[2,1024,384]{2,1,0:T(8,128)(2,1)} %all-gather.7.cloned.1.call-done), kind=kOutput, calls=%fused_computation.7 | convolution fusion | flops 855638016 | bytes 5472256 | tf_op jit(solution)/shard_map/encd,edf->encf/dot_general | solution.py:19
  91.0 33.5 %all-gather.9.cloned.1.call-done = bf16[2,384,1024]{2,1,0:T(8,128)(2,1)} async-done(((bf16[2,96,1024]{2,1,0:T(8,128)(2,1)}), bf16[2,384,1024]{2,1,0:T(8,128)(2,1)}) %all-gather.9.cloned.1.call-update) | async-done | bytes 1572880 | tf_op jit(solution)/shard_map/all_gather | solution.py:38
  124.5 3.9 %convolution_convert_fusion = bf16[2,8,68,1024]{3,2,1,0:T(8,128)(2,1)S(1)} fusion(bf16[2,384,1024]{2,1,0:T(8,128)(2,1)} %all-gather.9.cloned.1.call-done, f32[2,8,68,384]{3,2,1,0:T(8,128)} %fusion.2, f32[2,8,68,384]{3,2,1,0:T(8,128)} %fusion.4), kind=kOutput, calls=%fused_computation.15 | convolution fusion | flops 859258880 | bytes 7143424 | tf_op jit(solution)/shard_map/encf,efd->encd/dot_general | solution.py:22
  128.4 3.7 %copy.91 = bf16[2,8,68,1024]{3,0,2,1:T(2,128)(2,1)} copy(bf16[2,8,68,1024]{3,2,1,0:T(8,128)(2,1)S(1)} %convolution_convert_fusion) | data formatting | bytes 4456448 | tf_op jit(solution)/shard_map/convert_element_type | solution.py:24
  132.1 3.8 %all-to-all-start.1 = ((bf16[2,8,68,1024]{3,0,2,1:T(2,128)(2,1)}), bf16[2,8,68,1024]{3,0,2,1:T(2,128)(2,1)S(1)}, u32[]{:S(2)}, u32[]{:S(2)}) async-start(bf16[2,8,68,1024]{3,0,2,1:T(2,128)(2,1)} %copy.91), calls=%async_computation.1 | async-start | bytes 4456448 | tf_op jit(solution)/shard_map/all_to_all | solution.py:62
  137.1 26.9 %all-to-all-done.1 = bf16[2,8,68,1024]{3,0,2,1:T(2,128)(2,1)S(1)} async-done(((bf16[2,8,68,1024]{3,0,2,1:T(2,128)(2,1)}), bf16[2,8,68,1024]{3,0,2,1:T(2,128)(2,1)S(1)}, u32[]{:S(2)}, u32[]{:S(2)}) %all-to-all-start.1) | async-done | bytes 2228256 | tf_op jit(solution)/shard_map/all_to_all | solution.py:62
  164.0 2.1 copy.92
  166.1 2.6 reshape.128
  168.7 1.0 fusion.52
  171.0 37.8 %all-gather = bf16[32768]{0:T(1024)(128)(2,1)S(1)} all-gather(bf16[1024]{0:T(1024)(128)(2,1)S(1)} %multiply_convert_fusion.7), channel_id=2, replica_groups=mesh['dp'=4,'expert'=8] {'dp','expert'}, dimensions={0}, use_global_device_ids=true | all-gather | bytes 67584 | tf_op jit(solution)/shard_map/all_gather | solution.py:71
  210.3 36.9 %all-reduce = f32[32]{0:T(128)S(1)} all-reduce(f32[32]{0:T(128)S(1)} %dynamic-update-slice), channel_id=1, replica_groups=mesh['dp'=4,'expert'=8] {'dp','expert'}, use_global_device_ids=true, to_apply=%add | all-reduce | flops 32 | bytes 256
  249.4 1.7 multiply_convert_fusion
  251.1 4.5 %all-to-all-start.2 = ((bf16[16,1,68,1024]{3,2,1,0:T(8,128)(2,1)}), bf16[16,1,68,1024]{3,2,1,0:T(8,128)(2,1)}, u32[]{:S(2)}, u32[]{:S(2)}) async-start(bf16[16,1,68,1024]{3,2,1,0:T(8,128)(2,1)} %multiply_convert_fusion), calls=%async_computation.2 | async-start | bytes 4718592 | tf_op jit(solution)/shard_map/all_to_all | solution.py:113
  255.9 7.1 %gather_fusion.2 = s32[1024]{0:T(1024)S(1)} fusion(s32[128,16]{1,0:T(8,128)S(1)} %sub.31, s32[1024]{0:T(1024)S(1)} %reshape.148), kind=kCustom, calls=%fused_computation.2 | custom fusion | bytes 16384 | tf_op jit(solution)/shard_map/jit(take_along_axis)/gather | solution.py:45
  263.1 21.9 %all-to-all-done.2 = bf16[16,1,68,1024]{3,2,1,0:T(8,128)(2,1)} async-done(((bf16[16,1,68,1024]{3,2,1,0:T(8,128)(2,1)}), bf16[16,1,68,1024]{3,2,1,0:T(8,128)(2,1)}, u32[]{:S(2)}, u32[]{:S(2)}) %all-to-all-start.2) | async-done | bytes 2228256 | tf_op jit(solution)/shard_map/all_to_all | solution.py:113
  285.0 3.7 %fusion = f32[2,8,68,384]{3,2,1,0:T(8,128)S(1)} fusion(bf16[8,2,1,68,1024]{4,3,1,0,2:T(8,128)(2,1)} %bitcast.26, bf16[2,384,1024]{2,1,0:T(8,128)(2,1)} %all-gather.9.cloned.1.call-done), kind=kOutput, calls=%fused_computation.5 | convolution fusion | flops 855638016 | bytes 5472256 | tf_op jit(solution)/shard_map/encd,efd->encf/dot_general | solution.py:114
  288.7 1.6 fusion.12
  290.3 1.5 add_convert_fusion
  291.8 3.7 %copy.94 = bf16[2,8,68,1024]{3,0,2,1:T(2,128)(2,1)} copy(bf16[2,8,68,1024]{3,2,1,0:T(8,128)(2,1)S(1)} %add_convert_fusion) | data formatting | bytes 4456448 | tf_op jit(solution)/shard_map/convert_element_type | solution.py:126
  295.5 4.4 %all-to-all-start.3 = ((bf16[2,8,68,1024]{3,0,2,1:T(2,128)(2,1)}), bf16[2,8,68,1024]{3,0,2,1:T(2,128)(2,1)}, u32[]{:S(2)}, u32[]{:S(2)}) async-start(bf16[2,8,68,1024]{3,0,2,1:T(2,128)(2,1)} %copy.94), calls=%async_computation.3 | async-start | bytes 4456448 | tf_op jit(solution)/shard_map/all_to_all | solution.py:127
  300.3 1.8 convolution_reduce_fusion
  302.2 6.2 %gather_fusion.1 = f32[1024]{0:T(1024)S(1)} fusion(f32[1088]{0:T(1024)S(1)} %convolution_reduce_fusion, s32[1024]{0:T(1024)S(1)} %broadcast_clamp_fusion), kind=kCustom, calls=%fused_computation.1 | custom fusion | bytes 12288 | tf_op jit(solution)/shard_map/jit(_take)/gather | solution.py:107
  311.2 16.7 %all-to-all-done.3 = bf16[2,8,68,1024]{3,0,2,1:T(2,128)(2,1)} async-done(((bf16[2,8,68,1024]{3,0,2,1:T(2,128)(2,1)}), bf16[2,8,68,1024]{3,0,2,1:T(2,128)(2,1)}, u32[]{:S(2)}, u32[]{:S(2)}) %all-to-all-start.3) | async-done | bytes 2228256 | tf_op jit(solution)/shard_map/all_to_all | solution.py:127
  327.9 2.3 copy.95
  330.2 2.1 reshape.129
  332.3 2.9 fusion.17
  (65 shorter events, 10.3 us)
Async XLA Ops:
  7.2 42.2 %all-gather.5.cloned.1.call-start = ((), (), s32[]{:S(2)}) async-start(), calls=%async_computation.4 | async-start | bytes 1966080 | tf_op jit(solution)/shard_map/all_gather | solution.py:36
  7.9 79.1 %all-gather.7.cloned.1.call-start = ((), (), s32[]{:S(2)}) async-start(), calls=%async_computation.5 | async-start | bytes 1966080 | tf_op jit(solution)/shard_map/all_gather | solution.py:37
  12.8 34.6 %all-to-all-start = ((bf16[16,1,68,1024]{3,2,1,0:T(8,128)(2,1)}), bf16[16,1,68,1024]{3,2,1,0:T(8,128)(2,1)S(1)}, u32[]{:S(2)}, u32[]{:S(2)}) async-start(bf16[16,1,68,1024]{3,2,1,0:T(8,128)(2,1)} %convert_bitcast_fusion), calls=%async_computation | async-start | bytes 4718592 | tf_op jit(solution)/shard_map/all_to_all | solution.py:57
  18.0 106.5 %all-gather.9.cloned.1.call-start = ((), (), s32[]{:S(2)}) async-start(), calls=%async_computation.6 | async-start | bytes 1966080 | tf_op jit(solution)/shard_map/all_gather | solution.py:38
  132.1 3.8 %copy-start.1 = (s32[128,8]{0,1:T(8,128)S(1)}, s32[128,8]{0,1:T(8,128)}, u32[]{:S(2)}) copy-start(s32[128,8]{0,1:T(8,128)} %param.8) | copy-start | bytes 12292
  132.1 3.8 %copy-start.2 = (f32[128,8]{0,1:T(8,128)S(1)}, f32[128,8]{0,1:T(8,128)}, u32[]{:S(2)}) copy-start(f32[128,8]{0,1:T(8,128)} %param.9) | copy-start | bytes 12292
  132.1 4.3 %copy-start.3 = (s32[32]{0:T(128)S(1)}, s32[32]{0:T(128)}, u32[]{:S(2)}) copy-start(s32[32]{0:T(128)} %param.13) | copy-start | bytes 388
  132.1 4.9 %copy-start = (bf16[128,1024]{1,0:T(8,128)(2,1)S(1)}, bf16[128,1024]{1,0:T(8,128)(2,1)}, u32[]{:S(2)}) copy-start(bf16[128,1024]{1,0:T(8,128)(2,1)} %param.7) | copy-start | bytes 786436
  132.1 31.9 %all-to-all-start.1 = ((bf16[2,8,68,1024]{3,0,2,1:T(2,128)(2,1)}), bf16[2,8,68,1024]{3,0,2,1:T(2,128)(2,1)S(1)}, u32[]{:S(2)}, u32[]{:S(2)}) async-start(bf16[2,8,68,1024]{3,0,2,1:T(2,128)(2,1)} %copy.91), calls=%async_computation.1 | async-start | bytes 4456448 | tf_op jit(solution)/shard_map/all_to_all | solution.py:62
  251.1 33.8 %all-to-all-start.2 = ((bf16[16,1,68,1024]{3,2,1,0:T(8,128)(2,1)}), bf16[16,1,68,1024]{3,2,1,0:T(8,128)(2,1)}, u32[]{:S(2)}, u32[]{:S(2)}) async-start(bf16[16,1,68,1024]{3,2,1,0:T(8,128)(2,1)} %multiply_convert_fusion), calls=%async_computation.2 | async-start | bytes 4718592 | tf_op jit(solution)/shard_map/all_to_all | solution.py:113
  285.0 3.7 %copy-start.4 = (bf16[2,1024,384]{2,1,0:T(8,128)(2,1)S(1)}, bf16[2,1024,384]{2,1,0:T(8,128)(2,1)}, u32[]{:S(2)}) copy-start(bf16[2,1024,384]{2,1,0:T(8,128)(2,1)} %all-gather.5.cloned.1.call-done) | copy-start | bytes 4718596
  285.0 3.7 %copy-start.6 = (f32[2,8,68,384]{3,2,1,0:T(8,128)S(1)}, f32[2,8,68,384]{3,2,1,0:T(8,128)}, u32[]{:S(2)}) copy-start(f32[2,8,68,384]{3,2,1,0:T(8,128)} %fusion.4) | copy-start | bytes 5013508
  285.0 3.7 %copy-start.7 = (f32[2,8,68,384]{3,2,1,0:T(8,128)S(1)}, f32[2,8,68,384]{3,2,1,0:T(8,128)}, u32[]{:S(2)}) copy-start(f32[2,8,68,384]{3,2,1,0:T(8,128)} %fusion.2) | copy-start | bytes 5013508
  288.7 1.6 copy-start.5
  295.5 32.4 %all-to-all-start.3 = ((bf16[2,8,68,1024]{3,0,2,1:T(2,128)(2,1)}), bf16[2,8,68,1024]{3,0,2,1:T(2,128)(2,1)}, u32[]{:S(2)}, u32[]{:S(2)}) async-start(bf16[2,8,68,1024]{3,0,2,1:T(2,128)(2,1)} %copy.94), calls=%async_computation.3 | async-start | bytes 4456448 | tf_op jit(solution)/shard_map/all_to_all | solution.py:127
Sparse Core Ops, SparseCore 0:
  9.6 39.7 all-gather.4
  51.0 35.9 all-gather.6
  88.5 35.9 all-gather.8
where the time goes:
time: 344 us; the launch traced here: 343 us
  waiting for transfers between devices  165 us (48%)
  blocking collectives  74.6 us (22%)
  local copies, waits for them, and re-layouts  32 us (9%)
  matrix products  29.3 us (9%)
  starting transfers between devices  18 us (5%)
  between operations  17.9 us (5%)
  other arithmetic  5.82 us (2%)
    all_gather x1, blocking collectives, on_device(): gathered = lax.all_gather(embedding, ('dp', 'expert'), axis=0, tiled=True)  37.8 us
    unnamed x1, blocking collectives  36.9 us
    all_gather x1, waiting for transfers between devices, on_device(): lax.all_gather(w_down, 'dp', axis=1, tiled=True)  33.5 us
    all_gather x1, waiting for transfers between devices, on_device(): lax.all_gather(w_up, 'dp', axis=1, tiled=True)  33.5 us
    all_to_all x1, waiting for transfers between devices, on_device(): lax.all_to_all(outgoing, 'expert', split_axis=0, concat_axis=1, tiled=True)  28.7 us
    all_to_all x1, waiting for transfers between devices, on_device(): lax.all_to_all(out_here, 'expert', split_axis=1, concat_axis=0, tiled=True)  26.9 us
    all_to_all x1, waiting for transfers between devices, on_device(): lax.all_to_all(out_grad, 'expert', split_axis=0, concat_axis=1, tiled=True)  21.9 us
    all_to_all x1, waiting for transfers between devices, on_device(): lax.all_to_all(route_here, 'expert', split_axis=1, concat_axis=0, tiled=T...  16.7 us
  transfers between devices with their start and end apart: 7, of which 7 were waited for; matrix products, arithmetic and copies ran while one was open for 9% of the time, Pallas kernels for 0%

commit v1 on v0

--- a/solution.py
+++ b/solution.py
@@ -1,6 +1,8 @@
 import jax
 import jax.numpy as jnp
 from jax import lax
+from jax.experimental import pallas as pl
+from jax.experimental.pallas import tpu as pltpu
 from jax.sharding import PartitionSpec as P
 
 score_scale = 20.0
@@ -132,6 +134,441 @@
     return (contrast_loss, token_grad, gate_grad)
 
 
+mesh_ids = pl.DeviceIdType.MESH
+f32 = jnp.float32
+bf16 = jnp.bfloat16
+
+
+def split_dot(lhs, rhs, dims):
+    rows = lhs.shape[0]
+    high = lhs.astype(bf16)
+    low = (lhs - high.astype(f32)).astype(bf16)
+    both = lax.dot_general(
+        jnp.concatenate([high, low], axis=0), rhs, (dims, ((), ())), preferred_element_type=f32
+    )
+    return both[:rows] + both[rows:]
+
+
+def fused_kernel(
+    tok_ref, ids_ref, gv_ref, wg_ref, wu_ref, wd_ref, prow_ref, pcol_ref,
+    loss_ref, tg_ref, gg_ref,
+    tokb, gateb, wbuf, wpad, acc, hid, side, hbar, part, rsb, arb, pool, sgrad, vsend, vrecv, vown,
+    ggsend, ggrecv, rb, sibb, sumb, inb,
+    tok_s, tok_r, gate_s, gate_r, up_s, dn_s, w_r, hb_s, hb_r, rs_s, rs_r, ar_s, ar_r, ag_s, ag_r,
+    v_s, v_r, gg_s, gg_r, sib_s, sib_r, ret_s, ret_r,
+):
+    p = lax.axis_index("dp")
+    q = lax.axis_index("expert")
+    n_dp = wbuf.shape[0]
+    n_ex = gateb.shape[0]
+    rows, width = tok_ref.shape
+    ff = wg_ref.shape[2]
+    chips = n_ex // 2
+    chip = q // 2
+    core = q % 2
+    batch = n_dp * n_ex
+    own = p * n_ex + q
+    quarter = wbuf.shape[1]
+    ff_part = wd_ref.shape[1]
+    cols = width // n_ex
+    topk = ids_ref.shape[1]
+    experts = gateb.shape[2]
+
+    def ex_peer(i):
+        return (q + i) % n_ex
+
+    def ex_from(i):
+        return (q + n_ex - i) % n_ex
+
+    def dp_peer(i):
+        return (p + i) % n_dp
+
+    def dp_from(i):
+        return (p + n_dp - i) % n_dp
+
+    def send(src, dst, s_sem, r_sem, **where):
+        return pltpu.make_async_remote_copy(
+            src_ref=src, dst_ref=dst, send_sem=s_sem, recv_sem=r_sem,
+            device_id=(where.get("dp", p), where.get("ex", q)), device_id_type=mesh_ids,
+        )
+
+    barrier = pltpu.get_barrier_semaphore()
+    for i in range(1, n_ex):
+        pl.semaphore_signal(barrier, inc=1, device_id=(p, ex_peer(i)), device_id_type=mesh_ids)
+    for i in range(1, n_dp):
+        pl.semaphore_signal(barrier, inc=1, device_id=(dp_peer(i), q), device_id_type=mesh_ids)
+    for e in range(2):
+        wbuf[p, :, 2 * e * ff : (2 * e + 1) * ff] = wg_ref[e]
+        wbuf[p, :, (2 * e + 1) * ff : (2 * e + 2) * ff] = wu_ref[e]
+    pl.semaphore_wait(barrier, n_ex + n_dp - 2)
+
+    def up_copy(j):
+        return send(wbuf.at[j], wbuf.at[j], up_s.at[j], w_r.at[j], dp=jnp.minimum(p + 1, n_dp - 1))
+
+    def dn_copy(j):
+        return send(wbuf.at[j], wbuf.at[j], dn_s.at[j], w_r.at[j], dp=jnp.maximum(p - 1, 0))
+
+    @pl.when(p < n_dp - 1)
+    def _():
+        up_copy(p).start()
+
+    @pl.when(p > 0)
+    def _():
+        dn_copy(p).start()
+
+    own_rows = pl.ds(pl.multiple_of(q * rows, rows), rows)
+    tok_copies = []
+    for i in range(1, n_ex):
+        copy = send(tok_ref, tokb.at[own_rows, :], tok_s.at[i], tok_r.at[i], ex=ex_peer(i))
+        copy.start()
+        tok_copies.append(copy)
+    tokb[own_rows, :] = tok_ref[...]
+
+    expert_lane = lax.broadcasted_iota(jnp.int32, (rows, experts), 1)
+    gates = jnp.zeros((rows, experts), f32)
+    for k in range(topk):
+        gates = gates + jnp.where(ids_ref[:, k : k + 1] == expert_lane, gv_ref[:, k : k + 1], 0.0)
+    gateb[q] = gates
+    gate_copies = []
+    for i in range(1, n_ex):
+        copy = send(gateb.at[q], gateb.at[q], gate_s.at[i], gate_r.at[i], ex=ex_peer(i))
+        copy.start()
+        gate_copies.append(copy)
+
+    wpad[...] = jnp.zeros_like(wpad)
+    for e in range(2):
+        wpad[pl.ds(pl.multiple_of(e * ff + p * ff_part, 32), ff_part), :] = wd_ref[e]
+    ggsend[...] = jnp.zeros_like(ggsend)
+
+    for i in range(1, n_ex):
+        tok_copies[i - 1].wait_recv()
+        gate_copies[i - 1].wait_recv()
+
+    def multiply(j, first):
+        d_cols = pl.ds(pl.multiple_of(j * quarter, quarter), quarter)
+
+        def body(n, carry):
+            f_cols = pl.ds(pl.multiple_of(n * 256, 256), 256)
+            product = jnp.dot(tokb[:, d_cols], wbuf[j, :, f_cols], preferred_element_type=f32)
+            if first:
+                acc[:, f_cols] = product
+            else:
+                acc[:, f_cols] += product
+            return carry
+
+        lax.fori_loop(0, 4 * ff // 256, body, 0)
+
+    multiply(p, True)
+    for k in range(1, n_dp):
+        low, high = p - k, p + k
+
+        @pl.when(low >= 0)
+        def _():
+            up_copy(low).wait_recv()
+
+            @pl.when(p < n_dp - 1)
+            def _():
+                up_copy(low).start()
+
+        @pl.when(high < n_dp)
+        def _():
+            dn_copy(high).wait_recv()
+
+            @pl.when(p > 0)
+            def _():
+                dn_copy(high).start()
+
+        @pl.when(low >= 0)
+        def _():
+            multiply(low, False)
+
+        @pl.when(high < n_dp)
+        def _():
+            multiply(high, False)
+
+    def gate_column(s, e):
+        return jnp.sum(jnp.where(expert_lane == 2 * q + e, gateb[s], 0.0), axis=1, keepdims=True)
+
+    def forward(s, carry):
+        rs = pl.ds(pl.multiple_of(s * rows, rows), rows)
+        for e in range(2):
+            pre_gate = acc[rs, 2 * e * ff : (2 * e + 1) * ff]
+            pre_up = acc[rs, (2 * e + 1) * ff : (2 * e + 2) * ff]
+            hidden = (pre_gate * jax.nn.sigmoid(pre_gate) * pre_up).astype(bf16)
+            hid[rs, e * ff : (e + 1) * ff] = hidden
+            hbar[p, pl.ds(s, 1), e * ff : (e + 1) * ff] = jnp.sum(
+                gate_column(s, e) * hidden.astype(f32), axis=0, keepdims=True
+            )
+        return carry
+
+    lax.fori_loop(0, n_ex, forward, 0)
+    hb_copies = []
+    for i in range(1, n_dp):
+        copy = send(hbar.at[p], hbar.at[p], hb_s.at[i], hb_r.at[i], dp=dp_peer(i))
+        copy.start()
+        hb_copies.append(copy)
+
+    def factors(s, carry):
+        rs = pl.ds(pl.multiple_of(s * rows, rows), rows)
+        for e in range(2):
+            pre_gate = acc[rs, 2 * e * ff : (2 * e + 1) * ff]
+            pre_up = acc[rs, (2 * e + 1) * ff : (2 * e + 2) * ff]
+            activated, derivative = silu_parts(pre_gate)
+            gate = gate_column(s, e)
+            acc[rs, 2 * e * ff : (2 * e + 1) * ff] = gate * pre_up * derivative
+            acc[rs, (2 * e + 1) * ff : (2 * e + 2) * ff] = gate * activated
+        return carry
+
+    token_mean = jnp.sum(tok_ref[...].astype(f32), axis=0, keepdims=True) / rows
+    for copy in hb_copies:
+        copy.wait_recv()
+    own_row = lax.broadcasted_iota(jnp.int32, (batch, 1), 0) == own
+    part[...] = split_dot(
+        hbar[...].reshape(batch, 2 * ff), wpad[...], ((1,), (0,))
+    ) / rows + jnp.where(own_row, token_mean, 0.0)
+
+    def col_at(i):
+        return pl.ds(pl.multiple_of(i * cols, cols), cols)
+
+    rs_copies = []
+    for i in range(1, n_ex):
+        copy = send(part.at[:, col_at(ex_peer(i))], rsb.at[i], rs_s.at[i], rs_r.at[i], ex=ex_peer(i))
+        copy.start()
+        rs_copies.append(copy)
+    lax.fori_loop(0, n_ex // 2, factors, 0)
+    total = part[:, col_at(q)]
+    for i in range(1, n_ex):
+        rs_copies[i - 1].wait_recv()
+        total = total + rsb[i]
+    arb[p] = total
+    ar_copies = []
+    for i in range(1, n_dp):
+        copy = send(arb.at[p], arb.at[p], ar_s.at[i], ar_r.at[i], dp=dp_peer(i))
+        copy.start()
+        ar_copies.append(copy)
+    lax.fori_loop(n_ex // 2, n_ex, factors, 0)
+    for copy in ar_copies:
+        copy.wait_recv()
+    total = arb[0]
+    for j in range(1, n_dp):
+        total = total + arb[j]
+    pool[:, col_at(q)] = total
+    ag_copies = []
+    for i in range(1, n_ex):
+        copy = send(pool.at[:, col_at(q)], pool.at[:, col_at(q)], ag_s.at[i], ag_r.at[i], ex=ex_peer(i))
+        copy.start()
+        ag_copies.append(copy)
+    for copy in ag_copies:
+        copy.wait_recv()
+
+    pooled = pool[...]
+    inv_rms = lax.rsqrt(jnp.sum(pooled * pooled, axis=1, keepdims=True) / width + 1e-06)
+    embedding = (pooled * inv_rms).astype(bf16)
+    scale = score_scale / width
+    scores = scale * lax.dot_general(
+        embedding, embedding, (((1,), (1,)), ((), ())), preferred_element_type=f32
+    )
+    row_id = lax.broadcasted_iota(jnp.int32, (batch, batch), 0)
+    col_id = lax.broadcasted_iota(jnp.int32, (batch, batch), 1)
+    others = row_id != col_id
+    exps = jnp.where(others, jnp.exp(scores), 0.0)
+    log_total = jnp.log(jnp.sum(exps, axis=1, keepdims=True))
+    log_total_row = jnp.log(jnp.sum(exps, axis=0, keepdims=True))
+    hit = (pcol_ref[...] == col_id).astype(f32)
+    hit_turned = (prow_ref[...] == row_id).astype(f32)
+    partner_score = jnp.sum(scores * hit, axis=1, keepdims=True)
+    loss_ref[...] = jnp.sum(log_total - partner_score, axis=0, keepdims=True) / batch
+    both = (
+        jnp.where(others, jnp.exp(scores - log_total) + jnp.exp(scores - log_total_row), 0.0)
+        - hit
+        - hit_turned
+    )
+    embed_grad = scale * split_dot(both, embedding, ((1,), (0,)))
+    seq_grad = (
+        inv_rms * embed_grad
+        - inv_rms * inv_rms * inv_rms
+        * (jnp.sum(pooled * embed_grad, axis=1, keepdims=True) / width)
+        * pooled
+    )
+    sgrad[...] = seq_grad
+    vpart = split_dot(seq_grad, wpad[...], ((1,), (1,)))
+    for j in range(n_dp):
+        vsend[j] = vpart[j * n_ex : (j + 1) * n_ex]
+    v_copies = []
+    for i in range(1, n_dp):
+        copy = send(vsend.at[dp_peer(i)], vrecv.at[i], v_s.at[i], v_r.at[i], dp=dp_peer(i))
+        copy.start()
+        v_copies.append(copy)
+    total = vsend[p]
+    for i in range(1, n_dp):
+        v_copies[i - 1].wait_recv()
+        total = total + vrecv[i]
+    vown[...] = total
+
+    def sides(s):
+        rs = pl.ds(pl.multiple_of(s * rows, rows), rows)
+        for e in range(2):
+            v_row = vown[pl.ds(s, 1), e * ff : (e + 1) * ff]
+            for m in range(2):
+                c = slice((2 * e + m) * ff, (2 * e + m + 1) * ff)
+                side[rs, c] = (acc[rs, c] * v_row).astype(bf16)
+
+    sibling = chip * 2 + 1 - core
+    keep = pl.ds(pl.multiple_of(core * rows, rows), rows)
+    give = pl.ds(pl.multiple_of((1 - core) * rows, rows), rows)
+    order = list(range(1, chips)) + [0]
+
+    def sib_copy(i):
+        return send(rb.at[i, give, :], sibb.at[i], sib_s.at[i], sib_r.at[i], ex=sibling)
+
+    def ret_copy(i):
+        return send(sumb.at[i], inb.at[i], ret_s.at[i], ret_r.at[i], ex=((chip + i) % chips) * 2 + core)
+
+    def finish(i):
+        sib_copy(i).wait_recv()
+        summed = rb[i, keep, :].astype(f32) + sibb[i].astype(f32)
+        if i:
+            sumb[i] = summed.astype(bf16)
+            ret_copy(i).start()
+            return None
+        return summed
+
+    for step, i in enumerate(order):
+        target = (chip + i) % chips
+        sides(2 * target)
+        sides(2 * target + 1)
+        pair = pl.ds(pl.multiple_of(target * 2 * rows, 2 * rows), 2 * rows)
+
+        def back(j, carry, i=i, pair=pair):
+            rb[i, :, pl.ds(pl.multiple_of(j * quarter, quarter), quarter)] = lax.dot_general(
+                side[pair, :], wbuf[j], (((1,), (1,)), ((), ())), preferred_element_type=f32
+            ).astype(bf16)
+            return carry
+
+        lax.fori_loop(0, n_dp, back, 0)
+        sib_copy(i).start()
+        if step:
+            finish(order[step - 1])
+
+    lane = lax.broadcasted_iota(jnp.int32, (n_ex, n_ex * rows), 1)
+    block_diag = lane // rows == lax.broadcasted_iota(jnp.int32, (n_ex, n_ex * rows), 0)
+    for e in range(2):
+        dots = split_dot(
+            vown[:, e * ff : (e + 1) * ff], hid[:, e * ff : (e + 1) * ff], ((1,), (1,))
+        )
+        ggsend[e : e + 1, :] = jnp.sum(jnp.where(block_diag, dots, 0.0), axis=0, keepdims=True)
+
+    def seq_cols(i):
+        return pl.ds(pl.multiple_of(i * rows, rows), rows)
+
+    gg_copies = []
+    for i in range(1, n_ex):
+        copy = send(ggsend.at[:, seq_cols(ex_peer(i))], ggrecv.at[q], gg_s.at[i], gg_r.at[i], ex=ex_peer(i))
+        copy.start()
+        gg_copies.append(copy)
+    ggrecv[q] = ggsend[:, seq_cols(q)]
+    grad = finish(0) + sgrad[pl.ds(own, 1), :]
+    for copy in gg_copies:
+        copy.wait_recv()
+    all_dots = ggrecv[...].reshape(n_ex * 8, rows).T
+    dot_lane = lax.broadcasted_iota(jnp.int32, (rows, n_ex * 8), 1)
+    lane_expert = jnp.where(dot_lane % 8 < 2, dot_lane // 8 * 2 + dot_lane % 8, -1)
+    route_lane = lax.broadcasted_iota(jnp.int32, (rows, topk), 1)
+    result = jnp.zeros((rows, topk), f32)
+    for k in range(topk):
+        picked = jnp.sum(
+            jnp.where(ids_ref[:, k : k + 1] == lane_expert, all_dots, 0.0), axis=1, keepdims=True
+        )
+        result = jnp.where(route_lane == k, picked, result)
+    gg_ref[...] = result
+    for i in range(1, chips):
+        ret_copy(i).wait_recv()
+        grad = grad + inb[i].astype(f32)
+    tg_ref[...] = grad.astype(bf16)
+
+    for copies in (tok_copies, gate_copies, hb_copies, rs_copies, ar_copies, ag_copies, v_copies, gg_copies):
+        for copy in copies:
+            copy.wait_send()
+    for i in range(chips):
+        sib_copy(i).wait_send()
+        if i:
+            ret_copy(i).wait_send()
+    for k in range(n_dp):
+        low, high = p - k, p + k
+
+        @pl.when((low >= 0) & (p < n_dp - 1))
+        def _():
+            up_copy(low).wait_send()
+
+        @pl.when((high < n_dp) & (p > 0))
+        def _():
+            dn_copy(high).wait_send()
+
+
+def fused(tokens, expert_ids, gate_values, w_gate, w_up, w_down, partner):
+    rows, width = tokens.shape
+    topk = expert_ids.shape[1]
+    ff = w_gate.shape[2]
+    n_dp, n_ex = lax.axis_size("dp"), lax.axis_size("expert")
+    batch = n_dp * n_ex
+    all_rows = n_ex * rows
+    cols = width // n_ex
+    chips = n_ex // 2
+    dma = pltpu.SemaphoreType.DMA
+    vmem = pl.BlockSpec(memory_space=pltpu.VMEM)
+    loss, token_grad, gate_grad = pl.pallas_call(
+        fused_kernel,
+        out_shape=(
+            jax.ShapeDtypeStruct((1, 1), f32),
+            jax.ShapeDtypeStruct((rows, width), bf16),
+            jax.ShapeDtypeStruct((rows, topk), f32),
+        ),
+        in_specs=[vmem] * 8,
+        out_specs=(vmem, vmem, vmem),
+        scratch_shapes=[
+            pltpu.VMEM((all_rows, width), bf16),
+            pltpu.VMEM((n_ex, rows, 2 * n_ex), f32),
+            pltpu.VMEM((n_dp, width // n_dp, 4 * ff), bf16),
+            pltpu.VMEM((2 * ff, width), bf16),
+            pltpu.VMEM((all_rows, 4 * ff), f32),
+            pltpu.VMEM((all_rows, 2 * ff), bf16),
+            pltpu.VMEM((all_rows, 4 * ff), bf16),
+            pltpu.VMEM((n_dp, n_ex, 2 * ff), f32),
+            pltpu.VMEM((batch, width), f32),
+            pltpu.VMEM((n_ex, batch, cols), f32),
+            pltpu.VMEM((n_dp, batch, cols), f32),
+            pltpu.VMEM((batch, width), f32),
+            pltpu.VMEM((batch, width), f32),
+            pltpu.VMEM((n_dp, n_ex, 2 * ff), f32),
+            pltpu.VMEM((n_dp, n_ex, 2 * ff), f32),
+            pltpu.VMEM((n_ex, 2 * ff), f32),
+            pltpu.VMEM((8, all_rows), f32),
+            pltpu.VMEM((n_ex, 8, rows), f32),
+            pltpu.VMEM((chips, 2 * rows, width), bf16),
+            pltpu.VMEM((chips, rows, width), bf16),
+            pltpu.VMEM((chips, rows, width), bf16),
+            pltpu.VMEM((chips, rows, width), bf16),
+        ]
+        + [dma((n_ex,))] * 4
+        + [dma((n_dp,))] * 3
+        + [dma((n_dp,))] * 2
+        + [dma((n_ex,))] * 2
+        + [dma((n_dp,))] * 2
+        + [dma((n_ex,))] * 2
+        + [dma((n_dp,))] * 2
+        + [dma((n_ex,))] * 2
+        + [dma((chips,))] * 4,
+        compiler_params=pltpu.CompilerParams(
+            collective_id=0, has_side_effects=True, vmem_limit_bytes=48 * 1024 * 1024
+        ),
+    )(tokens, expert_ids, gate_values, w_gate, w_up, w_down, partner[None, :], partner[:, None])
+    return (loss[0, 0], token_grad, gate_grad)
+
+
+def fits_fused(mesh):
+    return mesh.shape["dp"] == 4 and mesh.shape["expert"] == 8
+
+
 def solution(mesh):
     placed = (
         P(("dp", "expert"), None),
@@ -143,7 +580,7 @@
         P(),
     )
     return jax.shard_map(
-        on_device,
+        fused if fits_fused(mesh) else on_device,
         mesh=mesh,
         in_specs=placed,
         out_specs=(P(), P(("dp", "expert"), None), P(("dp", "expert"), None)),

time: 344 us -> 129 us (0.38)
  waiting for transfers between devices: 165 us -> 0 us
  Pallas kernels: 0 us -> 118 us
  blocking collectives: 74.6 us -> 0 us
  matrix products: 29.3 us -> 0 us
  local copies, waits for them, and re-layouts: 32 us -> 7.42 us
  starting transfers between devices: 18 us -> 0 us
  between operations: 17.9 us -> 2.35 us
  other arithmetic: 5.82 us -> 0 us
    pallas_call x0 -> x1, Pallas kernels: none -> 118 us  [fused(): pl.pallas_call(fused_kernel, out_shape=(jax.ShapeDtypeStruct((1, 1), f32)...]
    all_to_all x4 -> x0, waiting for transfers between devices: 94.2 us -> none  [the longest x1 28.7 us: on_device(): lax.all_to_all(outgoing, 'expert', split_axis=0, concat_axis=1, tiled=True)]
    all_gather x3 -> x0, waiting for transfers between devices: 69 us -> none  [the longest x1 33.5 us: on_device(): lax.all_gather(w_down, 'dp', axis=1, tiled=True)]
    all_gather x1 -> x0, blocking collectives: 37.8 us -> none  [on_device(): gathered = lax.all_gather(embedding, ('dp', 'expert'), axis=0, tiled=True)]
    unnamed x1 -> x0, blocking collectives: 36.9 us -> none
    dot_general x13 -> x0, matrix products: 29.3 us -> none  [the longest x1 4.03 us: expert_forward(): jnp.einsum('encd,edf->encf', slot_piece, gate_full, preferred_element_typ...]
    all_to_all x4 -> x0, starting transfers between devices: 17.9 us -> none  [the longest x1 5.17 us: on_device(): lax.all_to_all(outgoing, 'expert', split_axis=0, concat_axis=1, tiled=True)]
    gather x9 -> x0, local copies, waits for them, and re-layouts: 14.3 us -> none  [the longest x5 7.39 us: on_device(): slot_rank = jnp.take_along_axis(before, expert_ids, axis=1)]
  transfers between devices with their start and end apart: 7 -> 0, of which waited for: 7 -> 0; matrix products, arithmetic and copies ran while one was open for 9% -> 0% of each run, Pallas kernels for 0% -> 0%
where the time goes in v1:
time: 129 us; the launch traced here: 128 us
  Pallas kernels  118 us (91%)
  local copies, waits for them, and re-layouts  7.42 us (6%)
  between operations  2.35 us (2%)
    pallas_call x1, Pallas kernels, fused(): pl.pallas_call(fused_kernel, out_shape=(jax.ShapeDtypeStruct((1, 1), f32)...  118 us
    unnamed x18, local copies, waits for them, and re-layouts  7.33 us

profile of v1, /device:TPU:0, one launch (start us, length us, event | category | flops | bytes accessed | tf_op | source)
XLA Modules:
  0.0 128.3 jit_solution(14065171829325889559)
XLA Ops:
  0.6 0.0 copy-start.4
  0.6 0.6 copy-done.4
  1.3 0.0 copy-start.5
  1.3 0.1 copy.12.pcol_ref
  1.4 0.6 copy-done.5
  2.0 0.0 copy-start.6
  2.0 0.1 copy.10.ids_ref
  2.1 0.6 copy-done.6
  2.7 0.1 copy.11.gv_ref
  2.8 0.0 copy-start
  2.8 1.0 copy-done
  3.8 0.0 copy-start.1
  3.8 1.0 copy-done.1
  4.8 0.0 copy-start.2
  4.8 1.0 copy-done.2
  5.8 0.0 copy-start.3
  5.8 0.9 copy-done.3
  6.7 118.5 %shard_map.94 = (f32[1,1]{1,0:T(1,128)}, bf16[128,1024]{1,0:T(8,128)(2,1)S(1)}, f32[128,8]{1,0:T(8,128)S(1)}) custom-call(bf16[128,1024]{1,0:T(8,128)(2,1)S(1)} %copy-done.3, s32[128,8]{1,0:T(8,128)S(1)} %copy.10.ids_ref, f32[128,8]{1,0:T(8,128)S(1)} %copy.11.gv_ref, bf16[2,256,384]{2,1,0:T(8,128)(2,1)S(1)} %copy-done, bf16[2,256,384]{2,1,0:T(8,128)(2,1)S(1)} %copy-done.1, ...), custom_call_target="tpu_custom_call" | custom-call | tf_op jit(solution)/shard_map/pallas_call | solution.py:519
  125.2 0.7 copy.13
  126.4 0.7 copy.17
Async XLA Ops:
  0.6 0.7 copy-start.4
  1.3 0.7 copy-start.5
  2.0 0.7 copy-start.6
  2.8 1.0 copy-start
  3.8 1.0 copy-start.1
  4.8 1.0 copy-start.2
  5.8 0.9 copy-start.3

commit v2 on v1

--- a/solution.py
+++ b/solution.py
@@ -150,11 +150,11 @@
 
 
 def fused_kernel(
-    tok_ref, ids_ref, gv_ref, wg_ref, wu_ref, wd_ref, prow_ref, pcol_ref,
+    tok_ref, ids_ref, gv_ref, wg_ref, wu_ref, wd_ref, prow_ref,
     loss_ref, tg_ref, gg_ref,
-    tokb, gateb, wbuf, wpad, acc, hid, side, hbar, part, rsb, arb, pool, sgrad, vsend, vrecv, vown,
+    tokb, gateb, gate_t, wbuf, wpad, acc, hid, side, hbar, part, rsb, arb, pool, sgrad, vsend, vrecv, vown,
     ggsend, ggrecv, rb, sibb, sumb, inb,
-    tok_s, tok_r, gate_s, gate_r, up_s, dn_s, w_r, hb_s, hb_r, rs_s, rs_r, ar_s, ar_r, ag_s, ag_r,
+    loc_s, tok_s, tok_r, gate_s, gate_r, up_s, dn_s, w_r, hb_s, hb_r, rs_s, rs_r, ar_s, ar_r, ag_s, ag_r,
     v_s, v_r, gg_s, gg_r, sib_s, sib_r, ret_s, ret_r,
 ):
     p = lax.axis_index("dp")
@@ -171,8 +171,8 @@
     quarter = wbuf.shape[1]
     ff_part = wd_ref.shape[1]
     cols = width // n_ex
-    topk = ids_ref.shape[1]
-    experts = gateb.shape[2]
+    topk = ids_ref.shape[0]
+    experts = gateb.shape[1]
 
     def ex_peer(i):
         return (q + i) % n_ex
@@ -197,37 +197,66 @@
         pl.semaphore_signal(barrier, inc=1, device_id=(p, ex_peer(i)), device_id_type=mesh_ids)
     for i in range(1, n_dp):
         pl.semaphore_signal(barrier, inc=1, device_id=(dp_peer(i), q), device_id_type=mesh_ids)
+    weight_loads = []
     for e in range(2):
-        wbuf[p, :, 2 * e * ff : (2 * e + 1) * ff] = wg_ref[e]
-        wbuf[p, :, (2 * e + 1) * ff : (2 * e + 2) * ff] = wu_ref[e]
+        for m, ref in enumerate((wg_ref, wu_ref)):
+            c = 2 * e + m
+            weight_loads.append(
+                pltpu.make_async_copy(ref.at[e], wbuf.at[p, :, c * ff : (c + 1) * ff], loc_s.at[c])
+            )
+    own_rows = pl.ds(pl.multiple_of(q * rows, rows), rows)
+    token_load = pltpu.make_async_copy(tok_ref, tokb.at[own_rows, :], loc_s.at[4])
+    for load in weight_loads:
+        load.start()
+    token_load.start()
+    wpad[...] = jnp.zeros_like(wpad)
+    down_loads = []
+    for e in range(2):
+        load = pltpu.make_async_copy(
+            wd_ref.at[e],
+            wpad.at[pl.ds(pl.multiple_of(e * ff + p * ff_part, 32), ff_part), :],
+            loc_s.at[5 + e],
+        )
+        load.start()
+        down_loads.append(load)
+    for load in weight_loads:
+        load.wait()
     pl.semaphore_wait(barrier, n_ex + n_dp - 2)
 
-    def up_copy(j):
-        return send(wbuf.at[j], wbuf.at[j], up_s.at[j], w_r.at[j], dp=jnp.minimum(p + 1, n_dp - 1))
-
-    def dn_copy(j):
-        return send(wbuf.at[j], wbuf.at[j], dn_s.at[j], w_r.at[j], dp=jnp.maximum(p - 1, 0))
-
-    @pl.when(p < n_dp - 1)
-    def _():
-        up_copy(p).start()
-
-    @pl.when(p > 0)
-    def _():
-        dn_copy(p).start()
-
-    own_rows = pl.ds(pl.multiple_of(q * rows, rows), rows)
+    half = quarter // 2
+
+    def piece(j, h):
+        return wbuf.at[j, h * half : (h + 1) * half, :]
+
+    def up_copy(j, h):
+        return send(
+            piece(j, h), piece(j, h), up_s.at[j, h], w_r.at[j, h], dp=jnp.minimum(p + 1, n_dp - 1)
+        )
+
+    def dn_copy(j, h):
+        return send(piece(j, h), piece(j, h), dn_s.at[j, h], w_r.at[j, h], dp=jnp.maximum(p - 1, 0))
+
+    for h in range(2):
+
+        @pl.when(p < n_dp - 1)
+        def _(h=h):
+            up_copy(p, h).start()
+
+        @pl.when(p > 0)
+        def _(h=h):
+            dn_copy(p, h).start()
+
+    token_load.wait()
     tok_copies = []
     for i in range(1, n_ex):
-        copy = send(tok_ref, tokb.at[own_rows, :], tok_s.at[i], tok_r.at[i], ex=ex_peer(i))
+        copy = send(tokb.at[own_rows, :], tokb.at[own_rows, :], tok_s.at[i], tok_r.at[i], ex=ex_peer(i))
         copy.start()
         tok_copies.append(copy)
-    tokb[own_rows, :] = tok_ref[...]
-
-    expert_lane = lax.broadcasted_iota(jnp.int32, (rows, experts), 1)
-    gates = jnp.zeros((rows, experts), f32)
+
+    expert_row = lax.broadcasted_iota(jnp.int32, (experts, rows), 0)
+    gates = jnp.zeros((experts, rows), f32)
     for k in range(topk):
-        gates = gates + jnp.where(ids_ref[:, k : k + 1] == expert_lane, gv_ref[:, k : k + 1], 0.0)
+        gates = gates + jnp.where(ids_ref[k : k + 1, :] == expert_row, gv_ref[k : k + 1, :], 0.0)
     gateb[q] = gates
     gate_copies = []
     for i in range(1, n_ex):
@@ -235,14 +264,9 @@
         copy.start()
         gate_copies.append(copy)
 
-    wpad[...] = jnp.zeros_like(wpad)
-    for e in range(2):
-        wpad[pl.ds(pl.multiple_of(e * ff + p * ff_part, 32), ff_part), :] = wd_ref[e]
     ggsend[...] = jnp.zeros_like(ggsend)
-
-    for i in range(1, n_ex):
-        tok_copies[i - 1].wait_recv()
-        gate_copies[i - 1].wait_recv()
+    for load in down_loads:
+        load.wait()
 
     def multiply(j, first):
         d_cols = pl.ds(pl.multiple_of(j * quarter, quarter), quarter)
@@ -258,25 +282,28 @@
 
         lax.fori_loop(0, 4 * ff // 256, body, 0)
 
-    multiply(p, True)
-    for k in range(1, n_dp):
+    def pass_on(k):
         low, high = p - k, p + k
-
-        @pl.when(low >= 0)
-        def _():
-            up_copy(low).wait_recv()
-
-            @pl.when(p < n_dp - 1)
-            def _():
-                up_copy(low).start()
-
-        @pl.when(high < n_dp)
-        def _():
-            dn_copy(high).wait_recv()
-
-            @pl.when(p > 0)
-            def _():
-                dn_copy(high).start()
+        for h in range(2):
+
+            @pl.when(low >= 0)
+            def _(h=h):
+                up_copy(low, h).wait_recv()
+
+                @pl.when(p < n_dp - 1)
+                def _():
+                    up_copy(low, h).start()
+
+            @pl.when(high < n_dp)
+            def _(h=h):
+                dn_copy(high, h).wait_recv()
+
+                @pl.when(p > 0)
+                def _():
+                    dn_copy(high, h).start()
+
+    def multiply_step(k):
+        low, high = p - k, p + k
 
         @pl.when(low >= 0)
         def _():
@@ -286,8 +313,22 @@
         def _():
             multiply(high, False)
 
+    pass_on(1)
+    for i in range(1, n_ex):
+        tok_copies[i - 1].wait_recv()
+        gate_copies[i - 1].wait_recv()
+    for s in range(n_ex):
+        gate_t[s] = gateb[s].T
+    multiply(p, True)
+    multiply_step(1)
+    for k in range(2, n_dp):
+        pass_on(k)
+        multiply_step(k)
+
+    expert_lane = lax.broadcasted_iota(jnp.int32, (rows, experts), 1)
+
     def gate_column(s, e):
-        return jnp.sum(jnp.where(expert_lane == 2 * q + e, gateb[s], 0.0), axis=1, keepdims=True)
+        return jnp.sum(jnp.where(expert_lane == 2 * q + e, gate_t[s], 0.0), axis=1, keepdims=True)
 
     def forward(s, carry):
         rs = pl.ds(pl.multiple_of(s * rows, rows), rows)
@@ -319,7 +360,7 @@
             acc[rs, (2 * e + 1) * ff : (2 * e + 2) * ff] = gate * activated
         return carry
 
-    token_mean = jnp.sum(tok_ref[...].astype(f32), axis=0, keepdims=True) / rows
+    token_mean = jnp.sum(tokb[own_rows, :].astype(f32), axis=0, keepdims=True) / rows
     for copy in hb_copies:
         copy.wait_recv()
     own_row = lax.broadcasted_iota(jnp.int32, (batch, 1), 0) == own
@@ -374,10 +415,10 @@
     exps = jnp.where(others, jnp.exp(scores), 0.0)
     log_total = jnp.log(jnp.sum(exps, axis=1, keepdims=True))
     log_total_row = jnp.log(jnp.sum(exps, axis=0, keepdims=True))
-    hit = (pcol_ref[...] == col_id).astype(f32)
     hit_turned = (prow_ref[...] == row_id).astype(f32)
-    partner_score = jnp.sum(scores * hit, axis=1, keepdims=True)
-    loss_ref[...] = jnp.sum(log_total - partner_score, axis=0, keepdims=True) / batch
+    hit = hit_turned.T
+    partner_score = jnp.sum(scores * hit_turned, axis=0, keepdims=True)
+    loss_ref[...] = jnp.sum(log_total_row - partner_score, axis=1, keepdims=True) / batch
     both = (
         jnp.where(others, jnp.exp(scores - log_total) + jnp.exp(scores - log_total_row), 0.0)
         - hit
@@ -470,17 +511,13 @@
     grad = finish(0) + sgrad[pl.ds(own, 1), :]
     for copy in gg_copies:
         copy.wait_recv()
-    all_dots = ggrecv[...].reshape(n_ex * 8, rows).T
-    dot_lane = lax.broadcasted_iota(jnp.int32, (rows, n_ex * 8), 1)
-    lane_expert = jnp.where(dot_lane % 8 < 2, dot_lane // 8 * 2 + dot_lane % 8, -1)
-    route_lane = lax.broadcasted_iota(jnp.int32, (rows, topk), 1)
-    result = jnp.zeros((rows, topk), f32)
+    all_dots = ggrecv[...].reshape(n_ex * 8, rows)
+    dot_row = lax.broadcasted_iota(jnp.int32, (n_ex * 8, 1), 0)
+    row_expert = jnp.where(dot_row % 8 < 2, dot_row // 8 * 2 + dot_row % 8, -1)
     for k in range(topk):
-        picked = jnp.sum(
-            jnp.where(ids_ref[:, k : k + 1] == lane_expert, all_dots, 0.0), axis=1, keepdims=True
+        gg_ref[k : k + 1, :] = jnp.sum(
+            jnp.where(ids_ref[k : k + 1, :] == row_expert, all_dots, 0.0), axis=0, keepdims=True
         )
-        result = jnp.where(route_lane == k, picked, result)
-    gg_ref[...] = result
     for i in range(1, chips):
         ret_copy(i).wait_recv()
         grad = grad + inb[i].astype(f32)
@@ -496,13 +533,15 @@
     for k in range(n_dp):
         low, high = p - k, p + k
 
-        @pl.when((low >= 0) & (p < n_dp - 1))
-        def _():
-            up_copy(low).wait_send()
-
-        @pl.when((high < n_dp) & (p > 0))
-        def _():
-            dn_copy(high).wait_send()
+        for h in range(2):
+
+            @pl.when((low >= 0) & (p < n_dp - 1))
+            def _(h=h):
+                up_copy(low, h).wait_send()
+
+            @pl.when((high < n_dp) & (p > 0))
+            def _(h=h):
+                dn_copy(high, h).wait_send()
 
 
 def fused(tokens, expert_ids, gate_values, w_gate, w_up, w_down, partner):
@@ -516,17 +555,19 @@
     chips = n_ex // 2
     dma = pltpu.SemaphoreType.DMA
     vmem = pl.BlockSpec(memory_space=pltpu.VMEM)
+    hbm = pl.BlockSpec(memory_space=pl.ANY)
     loss, token_grad, gate_grad = pl.pallas_call(
         fused_kernel,
         out_shape=(
             jax.ShapeDtypeStruct((1, 1), f32),
             jax.ShapeDtypeStruct((rows, width), bf16),
-            jax.ShapeDtypeStruct((rows, topk), f32),
+            jax.ShapeDtypeStruct((topk, rows), f32),
         ),
-        in_specs=[vmem] * 8,
+        in_specs=[hbm, vmem, vmem, hbm, hbm, hbm, vmem],
         out_specs=(vmem, vmem, vmem),
         scratch_shapes=[
             pltpu.VMEM((all_rows, width), bf16),
+            pltpu.VMEM((n_ex, 2 * n_ex, rows), f32),
             pltpu.VMEM((n_ex, rows, 2 * n_ex), f32),
             pltpu.VMEM((n_dp, width // n_dp, 4 * ff), bf16),
             pltpu.VMEM((2 * ff, width), bf16),
@@ -549,8 +590,9 @@
             pltpu.VMEM((chips, rows, width), bf16),
             pltpu.VMEM((chips, rows, width), bf16),
         ]
+        + [dma((8,))]
         + [dma((n_ex,))] * 4
-        + [dma((n_dp,))] * 3
+        + [dma((n_dp, 2))] * 3
         + [dma((n_dp,))] * 2
         + [dma((n_ex,))] * 2
         + [dma((n_dp,))] * 2
@@ -559,10 +601,10 @@
         + [dma((n_ex,))] * 2
         + [dma((chips,))] * 4,
         compiler_params=pltpu.CompilerParams(
-            collective_id=0, has_side_effects=True, vmem_limit_bytes=48 * 1024 * 1024
+            collective_id=0, has_side_effects=True, vmem_limit_bytes=60 * 1024 * 1024
         ),
-    )(tokens, expert_ids, gate_values, w_gate, w_up, w_down, partner[None, :], partner[:, None])
-    return (loss[0, 0], token_grad, gate_grad)
+    )(tokens, expert_ids.T, gate_values.T, w_gate, w_up, w_down, partner[None, :])
+    return (loss[0, 0], token_grad, gate_grad.T)
 
 
 def fits_fused(mesh):

time: 129 us -> 106 us (0.82)
  Pallas kernels: 118 us -> 102 us
  local copies, waits for them, and re-layouts: 7.42 us -> 2.27 us
    pallas_call x1, Pallas kernels: 118 us -> 102 us  [fused(): pl.pallas_call(fused_kernel, out_shape=(jax.ShapeDtypeStruct((1, 1), f32)...]
    unnamed x18 -> x4, local copies, waits for them, and re-layouts: 7.33 us -> 2.27 us
where the time goes in v2:
time: 106 us
  Pallas kernels  102 us (96%)
  between operations  2.46 us (2%)
  local copies, waits for them, and re-layouts  2.27 us (2%)
    pallas_call x1, Pallas kernels, fused(): pl.pallas_call(fused_kernel, out_shape=(jax.ShapeDtypeStruct((1, 1), f32)...  102 us
    unnamed x4, local copies, waits for them, and re-layouts  2.27 us

profile of v2, /device:TPU:0, one launch (start us, length us, event | category | flops | bytes accessed | tf_op | source)
XLA Modules:
  0.0 106.3 jit_solution(6592187227985941015)
XLA Ops:
  0.6 101.5 %shard_map.94 = (f32[1,1]{1,0:T(1,128)}, bf16[128,1024]{1,0:T(8,128)(2,1)}, f32[8,128]{1,0:T(8,128)}) custom-call(bf16[128,1024]{1,0:T(8,128)(2,1)} %tok_ref.1, s32[8,128]{1,0:T(8,128)} %bitcast.5, f32[8,128]{1,0:T(8,128)} %bitcast.6, bf16[2,256,384]{2,1,0:T(8,128)(2,1)} %wg_ref.1, bf16[2,256,384]{2,1,0:T(8,128)(2,1)} %wu_ref.1, ...), custom_call_target="tpu_custom_call" | custom-call | tf_op jit(solution)/shard_map/pallas_call | solution.py:559
  102.9 0.0 copy-start
  102.9 1.7 %copy.14 = bf16[128,1024]{1,0:T(8,128)(2,1)} copy(bf16[128,1024]{1,0:T(8,128)(2,1)} %get-tuple-element.13) | data formatting | bytes 524288
  104.6 0.0 copy-done
  104.6 0.6 copy.15
Async XLA Ops:
  102.9 1.7 %copy-start = (f32[8,128]{1,0:T(8,128)S(1)}, f32[8,128]{1,0:T(8,128)}, u32[]{:S(2)}) copy-start(f32[8,128]{1,0:T(8,128)} %get-tuple-element.8) | copy-start | bytes 12292

commit v3 on v2

--- a/solution.py
+++ b/solution.py
@@ -313,17 +313,18 @@
         def _():
             multiply(high, False)
 
-    pass_on(1)
+    for k in range(1, n_dp - 1):
+        pass_on(k)
     for i in range(1, n_ex):
         tok_copies[i - 1].wait_recv()
         gate_copies[i - 1].wait_recv()
     for s in range(n_ex):
         gate_t[s] = gateb[s].T
     multiply(p, True)
-    multiply_step(1)
-    for k in range(2, n_dp):
-        pass_on(k)
+    for k in range(1, n_dp - 1):
         multiply_step(k)
+    pass_on(n_dp - 1)
+    multiply_step(n_dp - 1)
 
     expert_lane = lax.broadcasted_iota(jnp.int32, (rows, experts), 1)
 
@@ -459,25 +460,39 @@
     give = pl.ds(pl.multiple_of((1 - core) * rows, rows), rows)
     order = list(range(1, chips)) + [0]
 
-    def sib_copy(i):
-        return send(rb.at[i, give, :], sibb.at[i], sib_s.at[i], sib_r.at[i], ex=sibling)
-
-    def ret_copy(i):
-        return send(sumb.at[i], inb.at[i], ret_s.at[i], ret_r.at[i], ex=((chip + i) % chips) * 2 + core)
-
-    def finish(i):
-        sib_copy(i).wait_recv()
-        summed = rb[i, keep, :].astype(f32) + sibb[i].astype(f32)
+    parts = 2
+    span = width // parts
+
+    def part_cols(h):
+        return slice(h * span, (h + 1) * span)
+
+    def sib_copy(i, h):
+        c = part_cols(h)
+        return send(rb.at[i, give, c], sibb.at[i, :, c], sib_s.at[i, h], sib_r.at[i, h], ex=sibling)
+
+    def ret_copy(i, h):
+        c = part_cols(h)
+        return send(
+            sumb.at[i, :, c], inb.at[i, :, c], ret_s.at[i, h], ret_r.at[i, h],
+            ex=((chip + i) % chips) * 2 + core,
+        )
+
+    def finish(i, h):
+        c = part_cols(h)
+        sib_copy(i, h).wait_recv()
+        summed = rb[i, keep, c].astype(f32) + sibb[i, :, c].astype(f32)
         if i:
-            sumb[i] = summed.astype(bf16)
-            ret_copy(i).start()
+            sumb[i, :, c] = summed.astype(bf16)
+            ret_copy(i, h).start()
             return None
         return summed
 
-    for step, i in enumerate(order):
+    units = [(i, h) for i in order for h in range(parts)]
+    for step, (i, h) in enumerate(units):
         target = (chip + i) % chips
-        sides(2 * target)
-        sides(2 * target + 1)
+        if h == 0:
+            sides(2 * target)
+            sides(2 * target + 1)
         pair = pl.ds(pl.multiple_of(target * 2 * rows, 2 * rows), 2 * rows)
 
         def back(j, carry, i=i, pair=pair):
@@ -486,10 +501,10 @@
             ).astype(bf16)
             return carry
 
-        lax.fori_loop(0, n_dp, back, 0)
-        sib_copy(i).start()
-        if step:
-            finish(order[step - 1])
+        lax.fori_loop(h * n_dp // parts, (h + 1) * n_dp // parts, back, 0)
+        sib_copy(i, h).start()
+        if step and units[step - 1][0]:
+            finish(*units[step - 1])
 
     lane = lax.broadcasted_iota(jnp.int32, (n_ex, n_ex * rows), 1)
     block_diag = lane // rows == lax.broadcasted_iota(jnp.int32, (n_ex, n_ex * rows), 0)
@@ -508,7 +523,6 @@
         copy.start()
         gg_copies.append(copy)
     ggrecv[q] = ggsend[:, seq_cols(q)]
-    grad = finish(0) + sgrad[pl.ds(own, 1), :]
     for copy in gg_copies:
         copy.wait_recv()
     all_dots = ggrecv[...].reshape(n_ex * 8, rows)
@@ -518,18 +532,22 @@
         gg_ref[k : k + 1, :] = jnp.sum(
             jnp.where(ids_ref[k : k + 1, :] == row_expert, all_dots, 0.0), axis=0, keepdims=True
         )
-    for i in range(1, chips):
-        ret_copy(i).wait_recv()
-        grad = grad + inb[i].astype(f32)
-    tg_ref[...] = grad.astype(bf16)
+    for h in range(parts):
+        c = part_cols(h)
+        grad = finish(0, h) + sgrad[pl.ds(own, 1), c]
+        for i in range(1, chips):
+            ret_copy(i, h).wait_recv()
+            grad = grad + inb[i, :, c].astype(f32)
+        tg_ref[:, c] = grad.astype(bf16)
 
     for copies in (tok_copies, gate_copies, hb_copies, rs_copies, ar_copies, ag_copies, v_copies, gg_copies):
         for copy in copies:
             copy.wait_send()
     for i in range(chips):
-        sib_copy(i).wait_send()
-        if i:
-            ret_copy(i).wait_send()
+        for h in range(parts):
+            sib_copy(i, h).wait_send()
+            if i:
+                ret_copy(i, h).wait_send()
     for k in range(n_dp):
         low, high = p - k, p + k
 
@@ -599,7 +617,7 @@
         + [dma((n_ex,))] * 2
         + [dma((n_dp,))] * 2
         + [dma((n_ex,))] * 2
-        + [dma((chips,))] * 4,
+        + [dma((chips, 2))] * 4,
         compiler_params=pltpu.CompilerParams(
             collective_id=0, has_side_effects=True, vmem_limit_bytes=60 * 1024 * 1024
         ),

time: 106 us -> 106 us (level)
  no operation moved by 1% of the time
where the time goes in v3:
time: 106 us; the launch traced here: 105 us
  Pallas kernels  101 us (95%)
  between operations  2.46 us (2%)
  local copies, waits for them, and re-layouts  2.27 us (2%)
    pallas_call x1, Pallas kernels, fused(): pl.pallas_call(fused_kernel, out_shape=(jax.ShapeDtypeStruct((1, 1), f32)...  101 us
    unnamed x4, local copies, waits for them, and re-layouts  2.27 us

profile of v3, /device:TPU:0, one launch (start us, length us, event | category | flops | bytes accessed | tf_op | source)
XLA Modules:
  0.0 105.5 jit_solution(10078002678732049113)
XLA Ops:
  0.6 100.8 %shard_map.94 = (f32[1,1]{1,0:T(1,128)}, bf16[128,1024]{1,0:T(8,128)(2,1)}, f32[8,128]{1,0:T(8,128)}) custom-call(bf16[128,1024]{1,0:T(8,128)(2,1)} %tok_ref.1, s32[8,128]{1,0:T(8,128)} %bitcast.5, f32[8,128]{1,0:T(8,128)} %bitcast.6, bf16[2,256,384]{2,1,0:T(8,128)(2,1)} %wg_ref.1, bf16[2,256,384]{2,1,0:T(8,128)(2,1)} %wu_ref.1, ...), custom_call_target="tpu_custom_call" | custom-call | tf_op jit(solution)/shard_map/pallas_call | solution.py:577
  102.1 0.0 copy-start
  102.1 1.7 %copy.14 = bf16[128,1024]{1,0:T(8,128)(2,1)} copy(bf16[128,1024]{1,0:T(8,128)(2,1)} %get-tuple-element.13) | data formatting | bytes 524288
  103.8 0.0 copy-done
  103.8 0.6 copy.15
Async XLA Ops:
  102.1 1.7 %copy-start = (f32[8,128]{1,0:T(8,128)S(1)}, f32[8,128]{1,0:T(8,128)}, u32[]{:S(2)}) copy-start(f32[8,128]{1,0:T(8,128)} %get-tuple-element.8) | copy-start | bytes 12292

commit v4 on v3

--- a/solution.py
+++ b/solution.py
@@ -223,7 +223,7 @@
         load.wait()
     pl.semaphore_wait(barrier, n_ex + n_dp - 2)
 
-    half = quarter // 2
+    half = quarter // 4
 
     def piece(j, h):
         return wbuf.at[j, h * half : (h + 1) * half, :]
@@ -236,7 +236,7 @@
     def dn_copy(j, h):
         return send(piece(j, h), piece(j, h), dn_s.at[j, h], w_r.at[j, h], dp=jnp.maximum(p - 1, 0))
 
-    for h in range(2):
+    for h in range(4):
 
         @pl.when(p < n_dp - 1)
         def _(h=h):
@@ -284,7 +284,7 @@
 
     def pass_on(k):
         low, high = p - k, p + k
-        for h in range(2):
+        for h in range(4):
 
             @pl.when(low >= 0)
             def _(h=h):
@@ -551,7 +551,7 @@
     for k in range(n_dp):
         low, high = p - k, p + k
 
-        for h in range(2):
+        for h in range(4):
 
             @pl.when((low >= 0) & (p < n_dp - 1))
             def _(h=h):
@@ -610,7 +610,7 @@
         ]
         + [dma((8,))]
         + [dma((n_ex,))] * 4
-        + [dma((n_dp, 2))] * 3
+        + [dma((n_dp, 4))] * 3
         + [dma((n_dp,))] * 2
         + [dma((n_ex,))] * 2
         + [dma((n_dp,))] * 2

time: 106 us -> 106 us (level)
  no operation moved by 1% of the time
where the time goes in v4:
time: 106 us
  Pallas kernels  101 us (95%)
  between operations  2.46 us (2%)
  local copies, waits for them, and re-layouts  2.27 us (2%)
    pallas_call x1, Pallas kernels, fused(): pl.pallas_call(fused_kernel, out_shape=(jax.ShapeDtypeStruct((1, 1), f32)...  101 us
    unnamed x4, local copies, waits for them, and re-layouts  2.27 us

profile of v4, /device:TPU:0, one launch (start us, length us, event | category | flops | bytes accessed | tf_op | source)
XLA Modules:
  0.0 105.7 jit_solution(17315883437911244466)
XLA Ops:
  0.6 101.0 %shard_map.94 = (f32[1,1]{1,0:T(1,128)}, bf16[128,1024]{1,0:T(8,128)(2,1)}, f32[8,128]{1,0:T(8,128)}) custom-call(bf16[128,1024]{1,0:T(8,128)(2,1)} %tok_ref.1, s32[8,128]{1,0:T(8,128)} %bitcast.5, f32[8,128]{1,0:T(8,128)} %bitcast.6, bf16[2,256,384]{2,1,0:T(8,128)(2,1)} %wg_ref.1, bf16[2,256,384]{2,1,0:T(8,128)(2,1)} %wu_ref.1, ...), custom_call_target="tpu_custom_call" | custom-call | tf_op jit(solution)/shard_map/pallas_call | solution.py:577
  102.3 0.0 copy-start
  102.3 1.7 %copy.14 = bf16[128,1024]{1,0:T(8,128)(2,1)} copy(bf16[128,1024]{1,0:T(8,128)(2,1)} %get-tuple-element.13) | data formatting | bytes 524288
  104.0 0.0 copy-done
  104.0 0.6 copy.15
Async XLA Ops:
  102.3 1.7 %copy-start = (f32[8,128]{1,0:T(8,128)S(1)}, f32[8,128]{1,0:T(8,128)}, u32[]{:S(2)}) copy-start(f32[8,128]{1,0:T(8,128)} %get-tuple-element.8) | copy-start | bytes 12292
